TPU v7x, 512 devices: a whole 4x4x16 slice. The times are simulated.
512 devices in a mesh: gx: 16 (over y, z_lo), gy: 32 (over x, z_hi, core).
Axes of the slice: x: 4, y: 4, z: 16 (z_hi: 4, z_lo: 4; z = z_hi * 4 + z_lo), core: 2. Of those that a mesh axis runs over, the one named last changes fastest.
Arguments:
- impedance: bfloat16 [16, 32, 2, 1024, 1024], P('gx', 'gy'), may hold values from -0.1875 to 0.1875
- sources: bfloat16 [16, 32, 2, 48, 1024], P('gx', 'gy'), may hold values from -6 to 6
- pattern: int32 [16, 32, 2, 2], P('gx', 'gy'), may hold values from 0 to 7
Outputs:
- combined: bfloat16 [16, 32, 2, 48, 1024], P('gx', 'gy')
All inputs are finite; a program needn't handle non-finite values.
Results may differ from a plain program's by a relative error of at most 0.02.
Values sent between devices are 32-bit elements; how exact they have to be, the bound alone decides.
A program may use at most 64 MiB of HBM per device.

v0:
```python
import functools

import jax
import jax.numpy as jnp
from jax import lax
from jax.experimental import pallas as pl
from jax.experimental.pallas import tpu as pltpu
from jax.sharding import PartitionSpec as P

COUPLING = 0.5
ROWS = 4
EARLY = 3
CROSSING = 10
WINDOW = 1
CHUNKS = 8
BLOCK = 256
MESH = pl.DeviceIdType.MESH


def coefficients(code, rows):
    flip = jnp.where(code >= 4, -1.0, 1.0).astype(jnp.float32)
    quarter = code % 4
    cos = jnp.where(quarter == 0, 1.0, jnp.where(quarter == 2, -1.0, 0.0)).astype(jnp.float32)
    sine = jnp.where(quarter == 1, 1.0, jnp.where(quarter == 3, -1.0, 0.0)).astype(jnp.float32)
    real = lax.broadcasted_iota(jnp.int32, (2 * rows, 128), 0) < rows
    return jnp.where(real, cos, cos * flip), jnp.where(real, -sine * flip, sine)


def kernel(
    nx, ny, groups, rows,
    k_hbm, s_ref, pat_ref, out_ref,
    k_ref, give_ref, take_ref, src_ref, coef_ref, sum_ref, in_x, in_y, fin_out, fin_in,
    k_sem, hand_send, hand_recv, send_x, send_y, recv_x, recv_y, fin_send, fin_recv,
):
    width = k_ref.shape[-1]
    nk = ny // 2
    cx = lax.axis_index("gx")
    cy = lax.axis_index("gy")
    ck = cy // 2
    core = cy % 2
    load = pltpu.make_async_copy(k_hbm, k_ref.at[core, 0], k_sem)
    load.start()

    last_depth = nx - 1 + 2 * (nk - 1)
    depth = (cx + 2 * ck, last_depth - cx - 2 * ck)
    step_of = (1, -1)
    has_x = (cx > 0, cx < nx - 1)
    has_y = (ck > 0, ck < nk - 1)

    def core_of(parity, side, along):
        mine = depth[side] + along
        gap = 2 * mine - last_depth
        moved = (gap > -CROSSING) & (gap < CROSSING) if side == 0 else gap < -last_depth
        return jnp.where(mine < EARLY, parity, jnp.where(moved, 0, 1))

    here = tuple(tuple(core_of(parity, side, 0) for side in range(2)) for parity in range(2))
    apart = tuple(here[0][side] != here[1][side] for side in range(2))

    barrier = pltpu.get_barrier_semaphore()
    pl.semaphore_signal(barrier, inc=1, device_id=(cx, cy + 1 - 2 * core), device_id_type=MESH)
    for side in range(2):
        back = -step_of[side]

        @pl.when(has_x[side])
        def _():
            for other in range(2):
                pl.semaphore_signal(
                    barrier, inc=1, device_id=(cx + back, 2 * ck + other), device_id_type=MESH
                )

        @pl.when(has_y[side])
        def _():
            for other in range(2):
                pl.semaphore_signal(
                    barrier, inc=1, device_id=(cx, 2 * (ck + back) + other), device_id_type=MESH
                )

    zero = jnp.zeros((groups, 2 * rows, width), jnp.float32)
    for side in range(2):
        @pl.when(jnp.logical_not(has_x[side]))
        def _():
            for parity in range(2):
                in_x[parity, side] = zero

        @pl.when(jnp.logical_not(has_y[side]))
        def _():
            in_y[side, side] = zero

        for parity in range(2):
            sum_ref[parity, side] = zero

    for side in range(2):
        for edge in range(2):
            own, swap = coefficients(pat_ref[side, edge], rows)
            coef_ref[core, side, edge, 0] = own
            coef_ref[core, side, edge, 1] = swap
    full = s_ref[...].astype(jnp.float32)
    for group in range(groups):
        part = slice(group * rows, (group + 1) * rows)
        src_ref[core, group] = jnp.concatenate([full[0, part], full[1, part]], axis=0)

    def transpose(parity):
        def block(index, carry):
            piece = index // (width // BLOCK)
            start = pl.multiple_of((index % (width // BLOCK)) * BLOCK, BLOCK)
            k_ref[parity, 1, piece, :, pl.ds(start, BLOCK)] = k_ref[
                parity, 0, piece, pl.ds(start, BLOCK), :
            ].T
            return carry

        lax.fori_loop(0, 2 * (width // BLOCK), block, 0)

    count = 1 + 2 * sum(jnp.where(flag, 1, 0) for flag in has_x + has_y)
    pl.semaphore_wait(barrier, count)

    def handover(src, dst, slot):
        return pltpu.make_async_remote_copy(
            src_ref=src, dst_ref=dst, send_sem=hand_send.at[slot], recv_sem=hand_recv.at[slot],
            device_id=(cx, 2 * ck + 1 - core), device_id_type=MESH,
        )

    chunk_rows = 2 * width // CHUNKS
    per_half = CHUNKS // 2

    def hand_parts(parity):
        return (
            handover(coef_ref.at[parity], coef_ref.at[parity], 0),
            handover(src_ref.at[parity], src_ref.at[parity], 1),
        )

    def chunk_copy(chunk):
        return handover(give_ref.at[chunk], take_ref.at[chunk], 2 + chunk)

    early = (depth[0] < EARLY, depth[1] < EARLY)
    met = (here[0][0] == 0) & jnp.logical_not(early[0]) | (here[0][1] == 0) & jnp.logical_not(early[1])
    gives = (core == 0) | met
    takes = (core == 1) | met
    turn_now = early[1] | (core == 1) & jnp.logical_not(early[0])

    @pl.when(gives)
    def _():
        for part in hand_parts(core):
            part.start()

    load.wait()

    @pl.when(turn_now)
    def _():
        transpose(core)

    def give():
        def send(chunk, carry):
            start = pl.multiple_of((chunk % per_half) * chunk_rows, chunk_rows)
            give_ref[chunk] = k_ref[
                core, 0, chunk // per_half, pl.ds(start, chunk_rows), :
            ].astype(jnp.float32)
            chunk_copy(chunk).start()
            return carry

        lax.fori_loop(0, CHUNKS, send, 0)

    def take():
        for part in hand_parts(1 - core):
            part.wait_recv()

        def receive(chunk, carry):
            chunk_copy(chunk).wait_recv()
            start = pl.multiple_of((chunk % per_half) * chunk_rows, chunk_rows)
            k_ref[1 - core, 0, chunk // per_half, pl.ds(start, chunk_rows), :] = take_ref[
                chunk
            ].astype(jnp.bfloat16)
            return carry

        lax.fori_loop(0, CHUNKS, receive, 0)

        @pl.when(jnp.where(core == 0, here[1][1], here[0][1]) == core)
        def _():
            transpose(1 - core)

        @pl.when(jnp.logical_not(turn_now) & (jnp.where(core == 0, here[0][1], here[1][1]) == core))
        def _():
            transpose(core)

    take_step = jnp.where(early[0] | early[1], min(EARLY + groups, last_depth - EARLY), 0)

    def copy_x(parity, side, group):
        step = step_of[side]
        there = core_of(parity, side, 1)
        return pltpu.make_async_remote_copy(
            src_ref=sum_ref.at[parity, side, group], dst_ref=in_x.at[parity, side, group],
            send_sem=send_x.at[parity, side, group], recv_sem=recv_x.at[parity, side, group],
            device_id=(cx + step, 2 * ck + there), device_id_type=MESH,
        )

    def copy_y(parity, side, group):
        step = step_of[side]
        if parity == side:
            target = (cx, 2 * ck + 1 - core)
        else:
            target = (cx, 2 * (ck + step) + core_of(1 - parity, side, 2))
        return pltpu.make_async_remote_copy(
            src_ref=sum_ref.at[parity, side, group], dst_ref=in_y.at[1 - parity, side, group],
            send_sem=send_y.at[parity, side, group], recv_sem=recv_y.at[1 - parity, side, group],
            device_id=target, device_id_type=MESH,
        )

    def fin_copy(group):
        return pltpu.make_async_remote_copy(
            src_ref=fin_out.at[group], dst_ref=fin_in.at[group],
            send_sem=fin_send.at[group], recv_sem=fin_recv.at[group],
            device_id=(cx, 2 * ck + 1 - core), device_id_type=MESH,
        )

    is_second = (depth[0] >= depth[1], depth[0] < depth[1])
    sends_x = (has_x[1], has_x[0])
    sends_y = (has_y[1], has_y[0])

    def exchanged(value):
        return jnp.concatenate([value[rows:], value[:rows]], axis=0)

    def wide(tile):
        return jnp.concatenate([tile] * (width // 128), axis=1)

    def advance(parity, side, group):
        to_x = copy_x(parity, side, group)
        to_y = copy_y(parity, side, group)
        from_y = copy_y(1 - parity, side, group)
        first = parity == side

        @pl.when(has_x[side])
        def _():
            to_x.wait_recv()

        @pl.when(has_y[side] if first else apart[side])
        def _():
            from_y.wait_recv()

        left = in_x[parity, side, group]
        down = in_y[parity, side, group]
        coef = [[wide(coef_ref[parity, side, edge, i]) for i in range(2)] for edge in range(2)]
        blend = (
            (coef[0][0] * left + coef[0][1] * exchanged(left))
            + (coef[1][0] * down + coef[1][1] * exchanged(down))
        )
        real = lax.broadcasted_iota(jnp.int32, blend.shape, 0) < rows
        other = exchanged(blend)
        turned = jnp.where(real, -other, other)
        contract = (((1,), (0,)), ((), ()))
        product = lax.dot_general(
            blend.astype(jnp.bfloat16), k_ref[parity, side, 0], contract,
            preferred_element_type=jnp.float32,
        ) + lax.dot_general(
            turned.astype(jnp.bfloat16), k_ref[parity, side, 1], contract,
            preferred_element_type=jnp.float32,
        )
        update = src_ref[parity, group] + COUPLING * product
        sum_ref[parity, side, group] = update

        @pl.when(apart[side] if first else sends_y[side])
        def _():
            if WINDOW < groups:
                @pl.when(group >= WINDOW)
                def _():
                    copy_y(parity, side, group - WINDOW).wait_send()

            to_y.start()

        @pl.when(sends_x[side])
        def _():
            if WINDOW < groups:
                @pl.when(group >= WINDOW)
                def _():
                    copy_x(parity, side, group - WINDOW).wait_send()

            to_x.start()

        if first:
            @pl.when(jnp.logical_not(apart[side]))
            def _():
                in_y[1 - parity, side, group] = update

        last = is_second[side] | (here[parity][1 - side] != core)

        @pl.when((core != parity) & last)
        def _():
            fin_out[group] = sum_ref[parity, 0, group] + sum_ref[parity, 1, group]
            fin_copy(group).start()

    def runs(parity, side):
        return core == here[parity][side]

    def section(step, carry):
        @pl.when(gives & (step == take_step))
        def _():
            give()

        @pl.when(takes & (step == take_step))
        def _():
            take()

        for side in (1, 0):
            group = step - depth[side]
            for parity in (side, 1 - side):
                @pl.when((group >= 0) & (group < groups) & runs(parity, side))
                def _():
                    advance(parity, side, group)

        return carry

    lax.fori_loop(0, last_depth + groups, section, 0)

    def store(parts):
        for half in range(2):
            out_ref[half] = jnp.concatenate(
                [part[half * rows : (half + 1) * rows] for part in parts], axis=0
            ).astype(jnp.bfloat16)

    def any_of(parity, where):
        return (here[parity][0] == where) | (here[parity][1] == where)

    for parity in range(2):
        awaits = any_of(parity, 1 - parity)

        @pl.when((core == parity) & awaits)
        def _():
            for group in range(groups):
                fin_copy(group).wait_recv()
            store([
                fin_in[group] + sum_ref[parity, 0, group] + sum_ref[parity, 1, group]
                for group in range(groups)
            ])

        @pl.when((core == parity) & jnp.logical_not(awaits))
        def _():
            store([sum_ref[parity, 0, group] + sum_ref[parity, 1, group] for group in range(groups)])

        @pl.when((core != parity) & awaits)
        def _():
            def sent(group, carry):
                fin_copy(group).wait_send()
                return carry

            lax.fori_loop(0, groups, sent, 0)

    @pl.when(gives)
    def _():
        for part in hand_parts(core):
            part.wait_send()

        def sent(chunk, carry):
            chunk_copy(chunk).wait_send()
            return carry

        lax.fori_loop(0, CHUNKS, sent, 0)

    def drain(group, carry):
        for side in range(2):
            for parity in range(2):
                @pl.when(runs(parity, side) & sends_x[side])
                def _():
                    copy_x(parity, side, group).wait_send()

                over = apart[side] if parity == side else sends_y[side]

                @pl.when(runs(parity, side) & over)
                def _():
                    copy_y(parity, side, group).wait_send()

        return carry

    lax.fori_loop(max(0, groups - WINDOW), groups, drain, 0)


def per_device(nx, ny, impedance, sources, pattern):
    _, _, _, count, width = sources.shape
    rows = ROWS
    groups = count // rows
    trace = (2, 2, groups, 2 * rows, width)
    vmem = pl.BlockSpec(memory_space=pltpu.VMEM)
    dma = pltpu.SemaphoreType.DMA
    result = pl.pallas_call(
        functools.partial(kernel, nx, ny, groups, rows),
        out_shape=jax.ShapeDtypeStruct((2, count, width), jnp.bfloat16),
        in_specs=[
            pl.BlockSpec(memory_space=pl.ANY),
            vmem,
            pl.BlockSpec(memory_space=pltpu.SMEM),
        ],
        out_specs=vmem,
        scratch_shapes=[
            pltpu.VMEM((2, 2, 2, width, width), jnp.bfloat16),
            pltpu.VMEM((CHUNKS, 2 * width // CHUNKS, width), jnp.float32),
            pltpu.VMEM((CHUNKS, 2 * width // CHUNKS, width), jnp.float32),
            pltpu.VMEM((2, groups, 2 * rows, width), jnp.float32),
            pltpu.VMEM((2, 2, 2, 2, 2 * rows, 128), jnp.float32),
            pltpu.VMEM(trace, jnp.float32),
            pltpu.VMEM(trace, jnp.float32),
            pltpu.VMEM(trace, jnp.float32),
            pltpu.VMEM((groups, 2 * rows, width), jnp.float32),
            pltpu.VMEM((groups, 2 * rows, width), jnp.float32),
            dma,
            dma((2 + CHUNKS,)),
            dma((2 + CHUNKS,)),
            dma((2, 2, groups)),
            dma((2, 2, groups)),
            dma((2, 2, groups)),
            dma((2, 2, groups)),
            dma((groups,)),
            dma((groups,)),
        ],
        compiler_params=pltpu.CompilerParams(
            collective_id=0, has_side_effects=True, vmem_limit_bytes=56 * 1024 * 1024
        ),
    )(impedance[0, 0], sources[0, 0], pattern[0, 0])
    return result[None, None]


def solution(mesh):
    in_specs = (
        P("gx", "gy", None, None, None),
        P("gx", "gy", None, None, None),
        P("gx", "gy", None, None),
    )
    out_specs = P("gx", "gy", None, None, None)
    body = functools.partial(per_device, mesh.shape["gx"], mesh.shape["gy"])
    return jax.shard_map(body, mesh=mesh, in_specs=in_specs, out_specs=out_specs, check_vma=False)
```

profile of v0, /device:TPU:1, one launch (start us, length us, event | category | flops | bytes accessed | tf_op | source)
XLA Modules:
  0.0 205.1 jit_solution(17369484755049673294)
XLA Ops:
  0.0 203.5 %shard_map.37 = bf16[2,48,1024]{2,1,0:T(8,128)(2,1)} custom-call(bf16[2,1024,1024]{2,1,0:T(8,128)(2,1)} %bitcast.4, bf16[2,48,1024]{2,1,0:T(8,128)(2,1)} %bitcast.6, s32[2,2]{1,0:T(2,128)} %bitcast.7), custom_call_target="tpu_custom_call" | custom-call | tf_op jit(solution)/shard_map/pallas_call | solution.py:381
  203.5 1.6 copy.5
where the time goes:
time: 209 us; the launch traced here: 205 us
  Pallas kernels  203 us (97%)
    pallas_call x1, Pallas kernels, per_device(): pl.pallas_call(functools.partial(kernel, nx, ny, groups, rows), out_shape...  203 us

commit v1 on v0

--- a/solution.py
+++ b/solution.py
@@ -13,6 +13,7 @@
 CROSSING = 10
 WINDOW = 1
 CHUNKS = 8
+PIECES = 2
 BLOCK = 256
 MESH = pl.DeviceIdType.MESH
 
@@ -28,9 +29,9 @@
 
 def kernel(
     nx, ny, groups, rows,
-    k_hbm, s_ref, pat_ref, out_ref,
-    k_ref, give_ref, take_ref, src_ref, coef_ref, sum_ref, in_x, in_y, fin_out, fin_in,
-    k_sem, hand_send, hand_recv, send_x, send_y, recv_x, recv_y, fin_send, fin_recv,
+    k_hbm, s_hbm, pat_ref, out_ref,
+    s_ref, k_ref, give_ref, take_ref, src_ref, coef_ref, sum_ref, in_x, in_y, fin_out, fin_in,
+    s_sem, k_sem, hand_send, hand_recv, send_x, send_y, recv_x, recv_y, fin_send, fin_recv,
 ):
     width = k_ref.shape[-1]
     nk = ny // 2
@@ -40,6 +41,8 @@
     core = cy % 2
     load = pltpu.make_async_copy(k_hbm, k_ref.at[core, 0], k_sem)
     load.start()
+    load_s = pltpu.make_async_copy(s_hbm, s_ref, s_sem)
+    load_s.start()
 
     last_depth = nx - 1 + 2 * (nk - 1)
     depth = (cx + 2 * ck, last_depth - cx - 2 * ck)
@@ -94,6 +97,7 @@
             own, swap = coefficients(pat_ref[side, edge], rows)
             coef_ref[core, side, edge, 0] = own
             coef_ref[core, side, edge, 1] = swap
+    load_s.wait()
     full = s_ref[...].astype(jnp.float32)
     for group in range(groups):
         part = slice(group * rows, (group + 1) * rows)
@@ -183,24 +187,35 @@
 
     take_step = jnp.where(early[0] | early[1], min(EARLY + groups, last_depth - EARLY), 0)
 
-    def copy_x(parity, side, group):
+    piece_width = width // PIECES
+
+    def columns(piece):
+        return slice(piece * piece_width, (piece + 1) * piece_width)
+
+    def copy_x(parity, side, group, piece):
         step = step_of[side]
         there = core_of(parity, side, 1)
+        slot = group * PIECES + piece
+        cut = columns(piece)
         return pltpu.make_async_remote_copy(
-            src_ref=sum_ref.at[parity, side, group], dst_ref=in_x.at[parity, side, group],
-            send_sem=send_x.at[parity, side, group], recv_sem=recv_x.at[parity, side, group],
+            src_ref=sum_ref.at[parity, side, group, :, cut],
+            dst_ref=in_x.at[parity, side, group, :, cut],
+            send_sem=send_x.at[parity, side, slot], recv_sem=recv_x.at[parity, side, slot],
             device_id=(cx + step, 2 * ck + there), device_id_type=MESH,
         )
 
-    def copy_y(parity, side, group):
+    def copy_y(parity, side, group, piece):
         step = step_of[side]
         if parity == side:
             target = (cx, 2 * ck + 1 - core)
         else:
             target = (cx, 2 * (ck + step) + core_of(1 - parity, side, 2))
+        slot = group * PIECES + piece
+        cut = columns(piece)
         return pltpu.make_async_remote_copy(
-            src_ref=sum_ref.at[parity, side, group], dst_ref=in_y.at[1 - parity, side, group],
-            send_sem=send_y.at[parity, side, group], recv_sem=recv_y.at[1 - parity, side, group],
+            src_ref=sum_ref.at[parity, side, group, :, cut],
+            dst_ref=in_y.at[1 - parity, side, group, :, cut],
+            send_sem=send_y.at[parity, side, slot], recv_sem=recv_y.at[1 - parity, side, slot],
             device_id=target, device_id_type=MESH,
         )
 
@@ -219,24 +234,19 @@
         return jnp.concatenate([value[rows:], value[:rows]], axis=0)
 
     def wide(tile):
-        return jnp.concatenate([tile] * (width // 128), axis=1)
-
-    def advance(parity, side, group):
-        to_x = copy_x(parity, side, group)
-        to_y = copy_y(parity, side, group)
-        from_y = copy_y(1 - parity, side, group)
-        first = parity == side
-
+        return jnp.concatenate([tile] * (piece_width // 128), axis=1)
+
+    def blended(parity, side, group, piece):
         @pl.when(has_x[side])
         def _():
-            to_x.wait_recv()
-
-        @pl.when(has_y[side] if first else apart[side])
-        def _():
-            from_y.wait_recv()
-
-        left = in_x[parity, side, group]
-        down = in_y[parity, side, group]
+            copy_x(parity, side, group, piece).wait_recv()
+
+        @pl.when(has_y[side] if parity == side else apart[side])
+        def _():
+            copy_y(1 - parity, side, group, piece).wait_recv()
+
+        left = in_x[parity, side, group, :, columns(piece)]
+        down = in_y[parity, side, group, :, columns(piece)]
         coef = [[wide(coef_ref[parity, side, edge, i]) for i in range(2)] for edge in range(2)]
         blend = (
             (coef[0][0] * left + coef[0][1] * exchanged(left))
@@ -245,39 +255,53 @@
         real = lax.broadcasted_iota(jnp.int32, blend.shape, 0) < rows
         other = exchanged(blend)
         turned = jnp.where(real, -other, other)
+        return blend.astype(jnp.bfloat16), turned.astype(jnp.bfloat16)
+
+    def product(parity, side, factors, piece, cut):
         contract = (((1,), (0,)), ((), ()))
-        product = lax.dot_general(
-            blend.astype(jnp.bfloat16), k_ref[parity, side, 0], contract,
-            preferred_element_type=jnp.float32,
-        ) + lax.dot_general(
-            turned.astype(jnp.bfloat16), k_ref[parity, side, 1], contract,
-            preferred_element_type=jnp.float32,
-        )
-        update = src_ref[parity, group] + COUPLING * product
-        sum_ref[parity, side, group] = update
-
-        @pl.when(apart[side] if first else sends_y[side])
-        def _():
-            if WINDOW < groups:
-                @pl.when(group >= WINDOW)
+        terms = [
+            lax.dot_general(
+                factor, k_ref[parity, side, half, columns(piece), cut], contract,
+                preferred_element_type=jnp.float32,
+            )
+            for half, factor in enumerate(factors)
+        ]
+        return terms[0] + terms[1]
+
+    def launch(parity, side, group, piece):
+        first = parity == side
+        for wanted, copy in (
+            (apart[side] if first else sends_y[side], copy_y), (sends_x[side], copy_x)
+        ):
+            @pl.when(wanted)
+            def _():
+                if WINDOW < groups:
+                    @pl.when(group >= WINDOW)
+                    def _():
+                        copy(parity, side, group - WINDOW, piece).wait_send()
+
+                copy(parity, side, group, piece).start()
+
+    def advance(parity, side, group):
+        first = parity == side
+        total = None
+        for piece in range(PIECES - 1):
+            factors = blended(parity, side, group, piece)
+            term = product(parity, side, factors, piece, slice(0, width))
+            total = term if total is None else total + term
+        factors = blended(parity, side, group, PIECES - 1)
+        for piece in range(PIECES):
+            cut = columns(piece)
+            term = product(parity, side, factors, PIECES - 1, cut)
+            if total is not None:
+                term = total[:, cut] + term
+            update = src_ref[parity, group, :, cut] + COUPLING * term
+            sum_ref[parity, side, group, :, cut] = update
+            launch(parity, side, group, piece)
+            if first:
+                @pl.when(jnp.logical_not(apart[side]))
                 def _():
-                    copy_y(parity, side, group - WINDOW).wait_send()
-
-            to_y.start()
-
-        @pl.when(sends_x[side])
-        def _():
-            if WINDOW < groups:
-                @pl.when(group >= WINDOW)
-                def _():
-                    copy_x(parity, side, group - WINDOW).wait_send()
-
-            to_x.start()
-
-        if first:
-            @pl.when(jnp.logical_not(apart[side]))
-            def _():
-                in_y[1 - parity, side, group] = update
+                    in_y[1 - parity, side, group, :, cut] = update
 
         last = is_second[side] | (here[parity][1 - side] != core)
 
@@ -356,15 +380,15 @@
     def drain(group, carry):
         for side in range(2):
             for parity in range(2):
-                @pl.when(runs(parity, side) & sends_x[side])
-                def _():
-                    copy_x(parity, side, group).wait_send()
-
                 over = apart[side] if parity == side else sends_y[side]
-
-                @pl.when(runs(parity, side) & over)
-                def _():
-                    copy_y(parity, side, group).wait_send()
+                for piece in range(PIECES):
+                    @pl.when(runs(parity, side) & sends_x[side])
+                    def _():
+                        copy_x(parity, side, group, piece).wait_send()
+
+                    @pl.when(runs(parity, side) & over)
+                    def _():
+                        copy_y(parity, side, group, piece).wait_send()
 
         return carry
 
@@ -383,11 +407,12 @@
         out_shape=jax.ShapeDtypeStruct((2, count, width), jnp.bfloat16),
         in_specs=[
             pl.BlockSpec(memory_space=pl.ANY),
-            vmem,
+            pl.BlockSpec(memory_space=pl.ANY),
             pl.BlockSpec(memory_space=pltpu.SMEM),
         ],
         out_specs=vmem,
         scratch_shapes=[
+            pltpu.VMEM((2, count, width), jnp.bfloat16),
             pltpu.VMEM((2, 2, 2, width, width), jnp.bfloat16),
             pltpu.VMEM((CHUNKS, 2 * width // CHUNKS, width), jnp.float32),
             pltpu.VMEM((CHUNKS, 2 * width // CHUNKS, width), jnp.float32),
@@ -399,12 +424,13 @@
             pltpu.VMEM((groups, 2 * rows, width), jnp.float32),
             pltpu.VMEM((groups, 2 * rows, width), jnp.float32),
             dma,
+            dma,
             dma((2 + CHUNKS,)),
             dma((2 + CHUNKS,)),
-            dma((2, 2, groups)),
-            dma((2, 2, groups)),
-            dma((2, 2, groups)),
-            dma((2, 2, groups)),
+            dma((2, 2, groups * PIECES)),
+            dma((2, 2, groups * PIECES)),
+            dma((2, 2, groups * PIECES)),
+            dma((2, 2, groups * PIECES)),
             dma((groups,)),
             dma((groups,)),
         ],

time: 209 us -> 203 us (0.971); the launches traced: 205 us -> 202 us
  Pallas kernels: 203 us -> 200 us
    pallas_call x1, Pallas kernels: 203 us -> 200 us  [per_device(): pl.pallas_call(functools.partial(kernel, nx, ny, groups, rows), out_shape...]
where the time goes in v1:
time: 203 us; the launch traced here: 202 us
  Pallas kernels  200 us (99%)
    pallas_call x1, Pallas kernels, per_device(): pl.pallas_call(functools.partial(kernel, nx, ny, groups, rows), out_shape...  200 us

profile of v1, /device:TPU:1, one launch (start us, length us, event | category | flops | bytes accessed | tf_op | source)
XLA Modules:
  0.0 201.8 jit_solution(3911605995084607264)
XLA Ops:
  0.0 200.2 %shard_map.37 = bf16[2,48,1024]{2,1,0:T(8,128)(2,1)} custom-call(bf16[2,1024,1024]{2,1,0:T(8,128)(2,1)} %bitcast.4, bf16[2,48,1024]{2,1,0:T(8,128)(2,1)} %bitcast.6, s32[2,2]{1,0:T(2,128)} %bitcast.7), custom_call_target="tpu_custom_call" | custom-call | tf_op jit(solution)/shard_map/pallas_call | solution.py:405
  200.2 1.6 copy.5

commit v2 on v1

--- a/solution.py
+++ b/solution.py
@@ -139,7 +139,8 @@
     met = (here[0][0] == 0) & jnp.logical_not(early[0]) | (here[0][1] == 0) & jnp.logical_not(early[1])
     gives = (core == 0) | met
     takes = (core == 1) | met
-    turn_now = early[1] | (core == 1) & jnp.logical_not(early[0])
+    unused = (core == 1) & (depth[1] == 0)
+    turn_now = jnp.logical_not(unused) & (early[1] | (core == 1) & jnp.logical_not(early[0]))
 
     @pl.when(gives)
     def _():
@@ -281,6 +282,27 @@
                         copy(parity, side, group - WINDOW, piece).wait_send()
 
                 copy(parity, side, group, piece).start()
+
+    def finish(parity, side, group):
+        last = is_second[side] | (here[parity][1 - side] != core)
+
+        @pl.when((core != parity) & last)
+        def _():
+            fin_out[group] = sum_ref[parity, 0, group] + sum_ref[parity, 1, group]
+            fin_copy(group).start()
+
+    def begin(parity, side, group):
+        for piece in range(PIECES):
+            cut = columns(piece)
+            update = src_ref[parity, group, :, cut]
+            sum_ref[parity, side, group, :, cut] = update
+            launch(parity, side, group, piece)
+
+            @pl.when(jnp.logical_not(apart[side]))
+            def _():
+                in_y[1 - parity, side, group, :, cut] = update
+
+        finish(parity, side, group)
 
     def advance(parity, side, group):
         first = parity == side
@@ -303,12 +325,7 @@
                 def _():
                     in_y[1 - parity, side, group, :, cut] = update
 
-        last = is_second[side] | (here[parity][1 - side] != core)
-
-        @pl.when((core != parity) & last)
-        def _():
-            fin_out[group] = sum_ref[parity, 0, group] + sum_ref[parity, 1, group]
-            fin_copy(group).start()
+        finish(parity, side, group)
 
     def runs(parity, side):
         return core == here[parity][side]
@@ -327,15 +344,25 @@
             for parity in (side, 1 - side):
                 @pl.when((group >= 0) & (group < groups) & runs(parity, side))
                 def _():
-                    advance(parity, side, group)
+                    if parity == side:
+                        @pl.when(depth[side] == 0)
+                        def _():
+                            begin(parity, side, group)
+
+                        @pl.when(depth[side] > 0)
+                        def _():
+                            advance(parity, side, group)
+                    else:
+                        advance(parity, side, group)
 
         return carry
 
     lax.fori_loop(0, last_depth + groups, section, 0)
 
-    def store(parts):
+    def store(start, parts):
+        at = slice(start * rows, (start + len(parts)) * rows)
         for half in range(2):
-            out_ref[half] = jnp.concatenate(
+            out_ref[half, at] = jnp.concatenate(
                 [part[half * rows : (half + 1) * rows] for part in parts], axis=0
             ).astype(jnp.bfloat16)
 
@@ -347,16 +374,19 @@
 
         @pl.when((core == parity) & awaits)
         def _():
-            for group in range(groups):
-                fin_copy(group).wait_recv()
-            store([
-                fin_in[group] + sum_ref[parity, 0, group] + sum_ref[parity, 1, group]
-                for group in range(groups)
-            ])
+            per = 16 // rows
+            for start in range(0, groups, per):
+                block = range(start, start + per)
+                for group in block:
+                    fin_copy(group).wait_recv()
+                store(start, [
+                    fin_in[group] + sum_ref[parity, 0, group] + sum_ref[parity, 1, group]
+                    for group in block
+                ])
 
         @pl.when((core == parity) & jnp.logical_not(awaits))
         def _():
-            store([sum_ref[parity, 0, group] + sum_ref[parity, 1, group] for group in range(groups)])
+            store(0, [sum_ref[parity, 0, group] + sum_ref[parity, 1, group] for group in range(groups)])
 
         @pl.when((core != parity) & awaits)
         def _():

time: 203 us -> 202 us (level)
  no operation moved by 1% of the time
where the time goes in v2:
time: 202 us
  Pallas kernels  200 us (99%)
    pallas_call x1, Pallas kernels, per_device(): pl.pallas_call(functools.partial(kernel, nx, ny, groups, rows), out_shape...  200 us

profile of v2, /device:TPU:1, one launch (start us, length us, event | category | flops | bytes accessed | tf_op | source)
XLA Modules:
  0.0 201.7 jit_solution(14621282700470249937)
XLA Ops:
  0.0 200.1 %shard_map.37 = bf16[2,48,1024]{2,1,0:T(8,128)(2,1)} custom-call(bf16[2,1024,1024]{2,1,0:T(8,128)(2,1)} %bitcast.4, bf16[2,48,1024]{2,1,0:T(8,128)(2,1)} %bitcast.6, s32[2,2]{1,0:T(2,128)} %bitcast.7), custom_call_target="tpu_custom_call" | custom-call | tf_op jit(solution)/shard_map/pallas_call | solution.py:435
  200.1 1.6 copy.5
